TPU v7x, 512 devices: a whole 4x8x8 slice. The times are simulated.
512 devices in a mesh: rep: 32 (over z, x), tp: 16 (over y, core).
Axes of the slice: x: 4, y: 8, z: 8, core: 2. Of those that a mesh axis runs over, the one named last changes fastest.
Arguments:
- queries: bfloat16 [1024, 4, 128, 576], P(('rep', 'tp')), parts along dimension 0, may hold values from -26 to 26
- latent_cache: bfloat16 [1024, 1024, 576], P(('rep', 'tp')), parts along dimension 0, may hold values from -4 to 4
- new_latent: bfloat16 [1024, 4, 576], P(('rep', 'tp')), parts along dimension 0, may hold values from -4 to 4
- cached_lengths: int32 [1024], P(('rep', 'tp')), parts along dimension 0, may hold values from 2 to 1024, as said below
- slot_rows: int32 [1024], P(('rep', 'tp')), parts along dimension 0, may hold values from 0 to 31, each once
- up_weight: bfloat16 [128, 512, 128], P('tp'), may hold values from -0.25 to 0.25
Outputs:
- attended: bfloat16 [1024, 4, 16384], P(('rep', 'tp')), parts along dimension 0
There are 32 independent parts, one for each index of `rep`. A program takes and returns all parts, laid end to end along the dimension named above; an argument that names none is the same for every part. Nothing has to cross between parts.
Inputs may be any that keep to these rules, and one draw needn't show every extreme that they name: `cached_lengths`: some slot has exactly 1024 cached positions. `slot_rows`: each row of the group is held by exactly one slot.
All inputs are finite; a program needn't handle non-finite values.
Results may differ from a plain program's by a relative error of at most 0.0052.
Values may be sent and summed in bfloat16 or wider, within the bound.
A program may use at most 64 MiB of HBM per device.

v0:
```python
import jax
import jax.numpy as jnp
from jax import lax
from jax.sharding import PartitionSpec as P

ROPE = 64
NOPE = 128


def attend_block(query_block, first_step, latent_cache, new_latent, cached_lengths, latent_dim):
    row_count, draft_count, head_count, embed_dim = query_block.shape
    total_steps = new_latent.shape[1]
    softmax_scale = (NOPE + ROPE) ** (-0.5)
    flat_queries = query_block.reshape(row_count, draft_count * head_count, embed_dim)
    old_scores = (
        jnp.einsum("rqe,rke->rqk", flat_queries, latent_cache, preferred_element_type=jnp.float32)
        * softmax_scale
    )
    new_scores = (
        jnp.einsum("rqe,rke->rqk", flat_queries, new_latent, preferred_element_type=jnp.float32)
        * softmax_scale
    )
    old_valid = jnp.arange(latent_cache.shape[1])[None, None, :] < cached_lengths[:, None, None]
    row_step = first_step + jnp.arange(draft_count * head_count) // head_count
    new_valid = jnp.arange(total_steps)[None, None, :] <= row_step[None, :, None]
    old_scores = jnp.where(old_valid, old_scores, -jnp.inf)
    new_scores = jnp.where(new_valid, new_scores, -jnp.inf)
    row_top = jnp.maximum(jnp.max(old_scores, axis=2), jnp.max(new_scores, axis=2))
    old_exp = jnp.exp(old_scores - row_top[:, :, None])
    new_exp = jnp.exp(new_scores - row_top[:, :, None])
    row_total = jnp.sum(old_exp, axis=2) + jnp.sum(new_exp, axis=2)
    mixed_sum = jnp.einsum(
        "rqk,rkl->rql",
        old_exp.astype(jnp.bfloat16),
        latent_cache[:, :, :latent_dim],
        preferred_element_type=jnp.float32,
    )
    mixed_sum = mixed_sum + jnp.einsum(
        "rqk,rkl->rql",
        new_exp.astype(jnp.bfloat16),
        new_latent[:, :, :latent_dim],
        preferred_element_type=jnp.float32,
    )
    latents = (mixed_sum / row_total[:, :, None]).astype(jnp.bfloat16)
    return latents.reshape(row_count, draft_count, head_count, latent_dim)


def per_device(queries, latent_cache, new_latent, cached_lengths, slot_rows, up_weight):
    row_count, draft_total, head_count, embed_dim = queries.shape
    latent_dim = up_weight.shape[1]
    value_dim = up_weight.shape[2]
    owners = lax.all_gather(slot_rows, "tp", axis=0, tiled=True)
    whole_rows = owners.shape[0]
    picker = (owners[None, :] == jnp.arange(whole_rows)[:, None]).astype(jnp.bfloat16)
    up_gathered = lax.all_gather(up_weight, "tp", axis=0, tiled=True)
    latents = attend_block(queries, 0, latent_cache, new_latent, cached_lengths, latent_dim)
    own_values = jnp.einsum(
        "rphl,hlv->rphv", latents, up_gathered, preferred_element_type=jnp.float32
    ).astype(jnp.bfloat16)
    arrived = lax.all_to_all(own_values, "tp", split_axis=2, concat_axis=0, tiled=True)
    ordered = jnp.einsum(
        "ab,bphv->aphv", picker, arrived, preferred_element_type=jnp.float32
    ).astype(jnp.bfloat16)
    result = lax.all_to_all(ordered, "tp", split_axis=0, concat_axis=2, tiled=True)
    return result.reshape(row_count, draft_total, head_count * value_dim)


def solution(mesh):
    return jax.shard_map(
        per_device,
        mesh=mesh,
        in_specs=(
            P(("rep", "tp"), None, None, None),
            P(("rep", "tp"), None, None),
            P(("rep", "tp"), None, None),
            P(("rep", "tp")),
            P(("rep", "tp")),
            P("tp", None, None),
        ),
        out_specs=P(("rep", "tp"), None, None),
        check_vma=False,
    )
```

profile of v0, /device:TPU:1, one launch (start us, length us, event | category | flops | bytes accessed | tf_op | source)
XLA Modules:
  0.0 167.3 jit_solution(5052884213417386817)
XLA Ops:
  6.5 0.0 copy-start
  6.5 0.0 all-gather.2.cloned.1.call-start
  6.5 0.7 all-gather.2.cloned.1.call-update
  7.3 1.0 iota_compare_fusion.2
  8.3 0.0 copy-done
  8.3 1.0 fusion.44
  9.3 2.0 %fusion.2 = (f32[2,512]{1,0:T(2,128)S(1)}, f32[2,512,1024]{2,1,0:T(8,128)S(1)}) fusion(pred[2,1024]{1,0:T(4,128)(4,1)S(1)} %iota_compare_fusion.2, bf16[2,1024,576]{1,2,0:T(8,128)(2,1)S(1)} %copy-done.1, bf16[2,4,128,576]{2,3,1,0:T(8,128)(2,1)S(1)} %copy-done), kind=kOutput, calls=%fused_computation.4 | convolution fusion | flops 1211104256 | bytes 7739392 | tf_op jit(solution)/shard_map/rqe,rke->rqk/dot_general | solution.py:16
  11.4 1.0 fusion.3
  12.4 0.0 copy-start.2
  12.4 1.4 fusion.5
  13.8 0.0 copy-done.2
  13.8 0.5 divide_convert_fusion
  14.3 98.8 %all-gather.2.cloned.1.call-done = bf16[128,512,128]{2,1,0:T(8,128)(2,1)} async-done(((bf16[8,512,128]{2,1,0:T(8,128)(2,1)}), bf16[128,512,128]{2,1,0:T(8,128)(2,1)}) %all-gather.2.cloned.1.call-update) | async-done | bytes 16777232 | tf_op jit(solution)/shard_map/all_gather | solution.py:55
  113.2 8.0 %fusion.19 = bf16[2,4,128,128]{3,1,0,2:T(4,128)(2,1)} fusion(bf16[128,512,128]{2,1,0:T(8,128)(2,1)} %all-gather.2.cloned.1.call-done, bf16[2,4,128,512]{3,2,1,0:T(8,128)(2,1)S(1)} %bitcast.50), kind=kOutput, calls=%fused_computation.20 | convolution fusion | flops 134348800 | bytes 18087936 | tf_op jit(solution)/shard_map/rphl,hlv->rphv/dot_general | solution.py:57
  121.2 4.7 %all-to-all-start = ((bf16[2,4,128,128]{3,1,0,2:T(4,128)(2,1)}), bf16[2,4,128,128]{3,1,0,2:T(4,128)(2,1)S(1)}, u32[]{:S(2)}, u32[]{:S(2)}) async-start(bf16[2,4,128,128]{3,1,0,2:T(4,128)(2,1)} %fusion.19), calls=%async_computation | async-start | bytes 524288 | tf_op jit(solution)/shard_map/all_to_all | solution.py:60
  125.9 1.3 dynamic-slice
  127.9 0.2 dynamic-update-slice
  128.2 12.1 %all-reduce = s32[32]{0:T(128)S(1)} all-reduce(s32[32]{0:T(128)S(1)} %dynamic-update-slice), channel_id=1, replica_groups=mesh['rep'=32,'tp'=16] {'tp'}, use_global_device_ids=true, to_apply=%add | all-reduce | flops 32 | bytes 256
  140.3 0.0 all-to-all-done
  140.3 0.2 copy.19
  140.5 0.2 convolution_convert_fusion
  140.7 0.1 copy.20
  140.8 18.8 %all_to_all.33 = bf16[32,4,8,128]{3,2,1,0:T(8,128)(2,1)S(1)} all-to-all(bf16[32,4,8,128]{3,2,1,0:T(8,128)(2,1)S(1)} %copy.20), channel_id=1, replica_groups=mesh['rep'=32,'tp'=16] {'tp'}, dimensions={0} | all-to-all | bytes 524288 | tf_op jit(solution)/shard_map/all_to_all | solution.py:64
  159.7 0.8 reshape.80
  (11 shorter events, 0.1 us)
Async XLA Ops:
  6.5 1.8 %copy-start = (bf16[2,4,128,576]{2,3,1,0:T(8,128)(2,1)S(1)}, bf16[2,4,128,576]{2,3,1,0:T(8,128)(2,1)}, u32[]{:S(2)}) copy-start(bf16[2,4,128,576]{2,3,1,0:T(8,128)(2,1)} %param.6) | copy-start | bytes 3538948
  6.5 2.8 %copy-start.1 = (bf16[2,1024,576]{1,2,0:T(8,128)(2,1)S(1)}, bf16[2,1024,576]{1,2,0:T(8,128)(2,1)}, u32[]{:S(2)}) copy-start(bf16[2,1024,576]{1,2,0:T(8,128)(2,1)} %param.7) | copy-start | bytes 7077892
  6.5 106.6 %all-gather.2.cloned.1.call-start = ((), (), s32[]{:S(2)}) async-start(), calls=%async_computation.2 | async-start | bytes 17825792 | tf_op jit(solution)/shard_map/all_gather | solution.py:55
  12.4 1.4 copy-start.2
  113.2 14.8 %copy-start.3 = (s32[2]{0:T(128)S(1)}, s32[2]{0:T(128)}, u32[]{:S(2)}) copy-start(s32[2]{0:T(128)} %param.10) | copy-start | bytes 28
  121.2 19.1 %all-to-all-start = ((bf16[2,4,128,128]{3,1,0,2:T(4,128)(2,1)}), bf16[2,4,128,128]{3,1,0,2:T(4,128)(2,1)S(1)}, u32[]{:S(2)}, u32[]{:S(2)}) async-start(bf16[2,4,128,128]{3,1,0,2:T(4,128)(2,1)} %fusion.19), calls=%async_computation | async-start | bytes 524288 | tf_op jit(solution)/shard_map/all_to_all | solution.py:60
Sparse Core Ops, SparseCore 0:
  9.5 103.6 all-gather.1
where the time goes:
time: 168 us; the launch traced here: 167 us
  waiting for transfers between devices  99.5 us (59%)
  blocking collectives  30.9 us (18%)
  between operations  14.2 us (8%)
  matrix products  13.1 us (8%)
  starting transfers between devices  4.73 us (3%)
  local copies, waits for them, and re-layouts  2.74 us (2%)
  other arithmetic  2.14 us (1%)
    all_gather x1, waiting for transfers between devices, per_device(): up_gathered = lax.all_gather(up_weight, 'tp', axis=0, tiled=True)  98.8 us
    all_to_all x1, blocking collectives, per_device(): lax.all_to_all(ordered, 'tp', split_axis=0, concat_axis=2, tiled=True)  18.8 us
    unnamed x1, blocking collectives  12.1 us
    dot_general x1, matrix products, per_device(): jnp.einsum('rphl,hlv->rphv', latents, up_gathered, preferred_element_type...  8 us
    all_to_all x1, starting transfers between devices, per_device(): lax.all_to_all(own_values, 'tp', split_axis=2, concat_axis=0, tiled=True)  4.73 us
  transfers between devices with their start and end apart: 2, of which 1 were waited for; matrix products, arithmetic and copies ran while one was open for 5% of the time, Pallas kernels for 0%

commit v1 on v0

v1 whole, which is shorter than its diff:
```python
import functools
import math

import jax
import jax.numpy as jnp
from jax import lax
from jax.experimental import pallas as pl
from jax.experimental.pallas import tpu as pltpu
from jax.sharding import PartitionSpec as P

ROPE = 64
NOPE = 128
MESH = pl.DeviceIdType.MESH

ORDER = (8, 9, 7, 10, 6, 11, 5, 12, 4, 13, 3, 14, 2, 15, 1, 0)
PER_GROUP = 4


def kernel(
    n,
    lengths_ref,
    rows_ref,
    q_hbm,
    cache_hbm,
    new_ref,
    up_hbm,
    out_ref,
    q_ref,
    cache_ref,
    up_ref,
    send1,
    recv1,
    send2,
    recv2,
    rows_out,
    rows_in,
    load_sem,
    rows_send_sem,
    rows_recv_sem,
    send1_sem,
    recv1_sem,
    own1_sem,
    send2_sem,
    recv2_sem,
    own2_sem,
):
    rep = lax.axis_index("rep")
    me = lax.axis_index("tp")
    slots, drafts, heads, _ = q_ref.shape
    ctx = cache_ref.shape[1]
    lat, values = up_hbm.shape[1], up_hbm.shape[2]
    own_heads = up_hbm.shape[0]
    pairs = drafts // 2
    groups = n // PER_GROUP
    per_block = slots * 2 * own_heads
    group_rows = PER_GROUP * per_block
    scale = (NOPE + ROPE) ** -0.5 * math.log2(math.e)

    barrier = pltpu.get_barrier_semaphore()
    for k in range(1, n):
        pl.semaphore_signal(barrier, inc=1, device_id=(rep, (me + k) % n), device_id_type=MESH)

    loads = []
    for b in range(slots):
        loads.append(
            (
                pltpu.make_async_copy(cache_hbm.at[b], cache_ref.at[b], load_sem.at[2 * b]),
                pltpu.make_async_copy(q_hbm.at[b], q_ref.at[b], load_sem.at[2 * b + 1]),
            )
        )
        for copy in loads[-1]:
            copy.start()
    up_loads = []
    for h in range(own_heads):
        copy = pltpu.make_async_copy(
            up_hbm.at[h], up_ref.at[:, pl.ds(h * values, values)], load_sem.at[2 * slots + h]
        )
        copy.start()
        up_loads.append(copy)

    lane = lax.broadcasted_iota(jnp.int32, (8, 128), 1)
    rows_out[...] = jnp.where((lane // (2 * own_heads)) % 2 == 0, rows_ref[0], rows_ref[1])

    def attend(b, pair):
        q = q_ref[b, pl.ds(2 * pair, 2)].reshape(2 * heads, q_ref.shape[3])
        keys = cache_ref[b]
        fresh = new_ref[b]
        contract = (((1,), (1,)), ((), ()))
        old = lax.dot_general(q, keys, contract, preferred_element_type=jnp.float32)
        new = lax.dot_general(q, fresh, contract, preferred_element_type=jnp.float32)
        position = lax.broadcasted_iota(jnp.int32, (1, ctx), 1)
        old = jnp.where(position < lengths_ref[b], old, -jnp.inf)
        step = 2 * pair + lax.broadcasted_iota(jnp.int32, new.shape, 0) // heads
        new = jnp.where(lax.broadcasted_iota(jnp.int32, new.shape, 1) <= step, new, -jnp.inf)
        top = jnp.maximum(jnp.max(old, axis=1, keepdims=True), jnp.max(new, axis=1, keepdims=True))
        old = jnp.exp2((old - top) * scale)
        new = jnp.exp2((new - top) * scale)
        total = jnp.sum(old, axis=1, keepdims=True) + jnp.sum(new, axis=1, keepdims=True)
        mixed = jnp.dot(old.astype(jnp.bfloat16), keys[:, :lat], preferred_element_type=jnp.float32)
        mixed = mixed + jnp.dot(new.astype(jnp.bfloat16), fresh[:, :lat], preferred_element_type=jnp.float32)
        latents = mixed * (1.0 / total)
        latents = latents.reshape(2, n, own_heads, lat)
        for d in range(n):
            block = jnp.concatenate([latents[0, d], latents[1, d]], axis=0)
            send1[pair, d, pl.ds(b * 2 * own_heads, 2 * own_heads), :] = block.astype(jnp.bfloat16)

    def send_first(pair):
        for p, k in enumerate(ORDER):
            to = (me + k) % n
            if k == 0:
                pltpu.make_async_copy(send1.at[pair, me], recv1.at[pair, p], own1_sem.at[pair]).start()
            else:
                pltpu.make_async_remote_copy(
                    src_ref=send1.at[pair, to],
                    dst_ref=recv1.at[pair, p],
                    send_sem=send1_sem.at[pair],
                    recv_sem=recv1_sem.at[pair, p // PER_GROUP],
                    device_id=(rep, to),
                    device_id_type=MESH,
                ).start()

    for pair in range(pairs):
        for b in range(slots):
            if pair == 0:
                for copy in loads[b]:
                    copy.wait()
            attend(b, pair)
        if pair == 0:
            pl.semaphore_wait(barrier, n - 1)
            for p, k in enumerate(ORDER):
                if k:
                    pltpu.make_async_remote_copy(
                        src_ref=rows_out,
                        dst_ref=rows_in.at[p],
                        send_sem=rows_send_sem,
                        recv_sem=rows_recv_sem,
                        device_id=(rep, (me + k) % n),
                        device_id_type=MESH,
                    ).start()
        send_first(pair)

    for copy in up_loads:
        copy.wait()
    pltpu.make_async_copy(rows_in.at[pl.ds(0, n - 1)], rows_in.at[pl.ds(0, n - 1)], rows_recv_sem).wait()
    rows_in[n - 1] = rows_out[...]

    out_lines = n * 16
    o = lax.broadcasted_iota(jnp.int32, (out_lines, group_rows), 0)
    i = lax.broadcasted_iota(jnp.int32, (out_lines, group_rows), 1)
    want = (o // 16) * 2 + (o // 2) % 2
    same_draft = (o % 2) == (i // own_heads) % 2
    source = lax.broadcasted_iota(jnp.int32, (1, group_rows), 1) // per_block
    picks = []
    for g in range(groups):
        held = rows_in[g * PER_GROUP][0:1]
        for s in range(1, PER_GROUP):
            held = jnp.where(source == s, rows_in[g * PER_GROUP + s][0:1], held)
        picks.append(jnp.where((want == held) & same_draft, 1.0, 0.0).astype(jnp.bfloat16))

    line_head = lax.broadcasted_iota(jnp.int32, (group_rows, values), 0) % own_heads
    quarter = (lax.broadcasted_iota(jnp.int32, (out_lines, 256), 0) // 4) % 4

    for pair in range(pairs):
        ordered = None
        for g in range(groups):
            first = g * PER_GROUP
            count = min(PER_GROUP, n - 1 - first)
            arrived = recv1.at[pair, pl.ds(first, count)]
            pltpu.make_async_copy(arrived, arrived, recv1_sem.at[pair, g]).wait()
            if count < PER_GROUP:
                pltpu.make_async_copy(send1.at[pair, me], recv1.at[pair, n - 1], own1_sem.at[pair]).wait()
            block = recv1[pair, pl.ds(first, PER_GROUP)].reshape(group_rows, lat)
            full = jnp.dot(block, up_ref[...], preferred_element_type=jnp.float32)
            kept = jnp.concatenate(
                [
                    jnp.where(line_head == h, full[:, h * values : (h + 1) * values], 0.0).astype(jnp.bfloat16)
                    for h in range(own_heads)
                ],
                axis=1,
            )
            part = jnp.dot(picks[g], kept, preferred_element_type=jnp.float32)
            ordered = part if ordered is None else ordered + part
        block = ordered[:, :256]
        for s in range(1, 4):
            block = jnp.where(quarter == s, ordered[:, s * 256 : (s + 1) * 256], block)
        send2[pair] = block.astype(jnp.bfloat16).reshape(n, 16, 256)
        columns = pl.ds(pl.multiple_of(me * 256, 256), 256)
        landing = recv2.at[pl.ds(pair * 16, 16), columns]
        for k in ORDER:
            to = (me + k) % n
            if k == 0:
                pltpu.make_async_copy(send2.at[pair, me], landing, own2_sem.at[pair]).start()
            else:
                pltpu.make_async_remote_copy(
                    src_ref=send2.at[pair, to],
                    dst_ref=landing,
                    send_sem=send2_sem.at[pair],
                    recv_sem=recv2_sem.at[pair],
                    device_id=(rep, to),
                    device_id_type=MESH,
                ).start()

    for pair in range(pairs):
        arrived = recv2.at[pl.ds(pair * 16, 16), pl.ds(0, (n - 1) * 256)]
        pltpu.make_async_copy(arrived, arrived, recv2_sem.at[pair]).wait()
        own = recv2.at[pl.ds(pair * 16, 16), pl.ds(pl.multiple_of(me * 256, 256), 256)]
        pltpu.make_async_copy(send2.at[pair, me], own, own2_sem.at[pair]).wait()

    lines = 4 * slots * drafts
    o = lax.broadcasted_iota(jnp.int32, (lines, pairs * 16), 0)
    i = lax.broadcasted_iota(jnp.int32, (lines, pairs * 16), 1)
    wanted = ((o % 4) // 2) * 16 + (o // 8) * 4 + ((o // 4) % 2) * 2 + o % 2
    place = jnp.where(i == wanted, 1.0, 0.0).astype(jnp.bfloat16)
    final = jnp.dot(place, recv2[...], preferred_element_type=jnp.float32)
    for s in range(n):
        for t in range(4):
            out_ref[:, pl.ds(s * 1024 + t * 256, 256)] = final[t * 8 : (t + 1) * 8, s * 256 : (s + 1) * 256].astype(
                jnp.bfloat16
            )

    pltpu.make_async_copy(rows_in.at[pl.ds(0, n - 1)], rows_in.at[pl.ds(0, n - 1)], rows_send_sem).wait()
    for pair in range(pairs):
        sent = send1.at[pair, pl.ds(0, n - 1)]
        pltpu.make_async_copy(sent, sent, send1_sem.at[pair]).wait()
        sent = send2.at[pair, pl.ds(0, n - 1)]
        pltpu.make_async_copy(sent, sent, send2_sem.at[pair]).wait()


def per_device(n, queries, latent_cache, new_latent, cached_lengths, slot_rows, up_weight):
    slots, drafts, heads, embed = queries.shape
    own_heads, lat, values = up_weight.shape
    ctx = latent_cache.shape[1]
    pairs = drafts // 2
    per_block = slots * 2 * own_heads
    smem = pl.BlockSpec(memory_space=pltpu.SMEM)
    vmem = pl.BlockSpec(memory_space=pltpu.VMEM)
    hbm = pl.BlockSpec(memory_space=pl.ANY)
    dma = pltpu.SemaphoreType.DMA
    bf16 = jnp.bfloat16
    out = pl.pallas_call(
        functools.partial(kernel, n),
        out_shape=jax.ShapeDtypeStruct((slots * drafts, heads * values), bf16),
        in_specs=[smem, smem, hbm, hbm, vmem, hbm],
        out_specs=vmem,
        scratch_shapes=[
            pltpu.VMEM((slots, drafts, heads, embed), bf16),
            pltpu.VMEM((slots, ctx, embed), bf16),
            pltpu.VMEM((lat, own_heads * values), bf16),
            pltpu.VMEM((pairs, n, per_block, lat), bf16),
            pltpu.VMEM((pairs, n, per_block, lat), bf16),
            pltpu.VMEM((pairs, n, 16, 256), bf16),
            pltpu.VMEM((pairs * 16, n * 256), bf16),
            pltpu.VMEM((8, 128), jnp.int32),
            pltpu.VMEM((n, 8, 128), jnp.int32),
            dma((2 * slots + own_heads,)),
            dma,
            dma,
            dma((pairs,)),
            dma((pairs, n // PER_GROUP)),
            dma((pairs,)),
            dma((pairs,)),
            dma((pairs,)),
            dma((pairs,)),
        ],
        compiler_params=pltpu.CompilerParams(collective_id=0, has_side_effects=True, vmem_limit_bytes=48 << 20),
    )(cached_lengths, slot_rows, queries, latent_cache, new_latent, up_weight)
    return out.reshape(slots, drafts, heads * values)


def solution(mesh):
    return jax.shard_map(
        functools.partial(per_device, mesh.shape["tp"]),
        mesh=mesh,
        in_specs=(
            P(("rep", "tp"), None, None, None),
            P(("rep", "tp"), None, None),
            P(("rep", "tp"), None, None),
            P(("rep", "tp")),
            P(("rep", "tp")),
            P("tp", None, None),
        ),
        out_specs=P(("rep", "tp"), None, None),
        check_vma=False,
    )
```

time: 168 us -> 52.5 us (0.31)
  waiting for transfers between devices: 99.5 us -> 0 us
  Pallas kernels: 0 us -> 43.3 us
  blocking collectives: 30.9 us -> 0 us
  between operations: 14.2 us -> 0.05 us
  matrix products: 13.1 us -> 0 us
  local copies, waits for them, and re-layouts: 2.74 us -> 8.87 us
  starting transfers between devices: 4.73 us -> 0 us
  other arithmetic: 2.14 us -> 0 us
    all_gather x1 -> x0, waiting for transfers between devices: 98.8 us -> none  [per_device(): up_gathered = lax.all_gather(up_weight, 'tp', axis=0, tiled=True)]
    pallas_call x0 -> x1, Pallas kernels: none -> 43.3 us  [per_device(): pl.pallas_call(functools.partial(kernel, n), out_shape=jax.ShapeDtypeStru...]
    all_to_all x1 -> x0, blocking collectives: 18.8 us -> none  [per_device(): lax.all_to_all(ordered, 'tp', split_axis=0, concat_axis=2, tiled=True)]
    dot_general x6 -> x0, matrix products: 13.1 us -> none  [the longest x1 8 us: per_device(): jnp.einsum('rphl,hlv->rphv', latents, up_gathered, preferred_element_type...]
    unnamed x1 -> x0, blocking collectives: 12.1 us -> none
    unnamed x11 -> x12, local copies, waits for them, and re-layouts: 1.6 us -> 8.07 us
    all_to_all x1 -> x0, starting transfers between devices: 4.73 us -> none  [per_device(): lax.all_to_all(own_values, 'tp', split_axis=2, concat_axis=0, tiled=True)]
  transfers between devices with their start and end apart: 2 -> 0, of which waited for: 1 -> 0; matrix products, arithmetic and copies ran while one was open for 5% -> 0% of each run, Pallas kernels for 0% -> 0%
where the time goes in v1:
time: 52.5 us; the launch traced here: 52.2 us
  Pallas kernels  43.3 us (82%)
  local copies, waits for them, and re-layouts  8.87 us (17%)
    pallas_call x1, Pallas kernels, per_device(): pl.pallas_call(functools.partial(kernel, n), out_shape=jax.ShapeDtypeStru...  43.3 us
    unnamed x12, local copies, waits for them, and re-layouts  8.07 us

profile of v1, /device:TPU:1, one launch (start us, length us, event | category | flops | bytes accessed | tf_op | source)
XLA Modules:
  0.0 52.2 jit_solution(661185084229570569)
XLA Ops:
  0.0 2.4 %copy.7.q_hbm = bf16[2,4,128,576]{3,2,1,0:T(8,128)(2,1)} copy(bf16[2,4,128,576]{2,3,1,0:T(8,128)(2,1)} %param.6) | data formatting | bytes 2359296 | tf_op args[0]
  2.4 0.0 copy-start.2
  2.4 0.0 copy-start.3
  2.4 0.0 copy-start.4
  2.4 3.1 %copy.8.cache_hbm = bf16[2,1024,576]{2,1,0:T(8,128)(2,1)S(1)} copy(bf16[2,1024,576]{1,2,0:T(8,128)(2,1)} %param.7) | data formatting | bytes 4718592 | tf_op args[1]
  5.5 0.0 copy-done.2
  5.5 0.0 copy-done.3
  5.6 0.0 copy-done.4
  5.6 0.0 copy-start
  5.6 1.3 %copy-done = bf16[2,4,128,576]{3,2,1,0:T(8,128)(2,1)S(1)} copy-done((bf16[2,4,128,576]{3,2,1,0:T(8,128)(2,1)S(1)}, bf16[2,4,128,576]{3,2,1,0:T(8,128)(2,1)}, u32[]{:S(2)}) %copy-start) | copy-done | bytes 1179672
  6.9 0.0 copy-start.1
  6.9 1.2 %copy-done.1 = bf16[8,512,128]{2,1,0:T(8,128)(2,1)S(1)} copy-done((bf16[8,512,128]{2,1,0:T(8,128)(2,1)S(1)}, bf16[8,512,128]{2,1,0:T(8,128)(2,1)}, u32[]{:S(2)}) %copy-start.1) | copy-done | bytes 1048600
  8.1 43.3 %shard_map.64 = bf16[8,16384]{1,0:T(8,128)(2,1)S(1)} custom-call(s32[2]{0:T(128)S(1)} %copy-done.3, s32[2]{0:T(128)S(1)} %copy-done.4, bf16[2,4,128,576]{3,2,1,0:T(8,128)(2,1)S(1)} %copy-done, bf16[2,1024,576]{2,1,0:T(8,128)(2,1)S(1)} %copy.8.cache_hbm, bf16[2,4,576]{2,1,0:T(4,128)(2,1)S(1)} %copy-done.2, bf16[8,512,128]{2,1,0:T(8,128)(2,1)S(1)} %copy-done.1), custom_call_target="tpu_custom_call" | custom-call | tf_op jit(solution)/shard_map/pallas_call | solution.py:240
  51.4 0.8 %reshape.3 = bf16[2,4,16384]{2,1,0:T(4,128)(2,1)} reshape(bf16[8,16384]{1,0:T(8,128)(2,1)S(1)} %shard_map.64) | data formatting | bytes 524288 | tf_op jit(solution)/shard_map/reshape | solution.py:267
Async XLA Ops:
  2.4 3.1 %copy-start.2 = (bf16[2,4,576]{2,1,0:T(4,128)(2,1)S(1)}, bf16[2,4,576]{2,1,0:T(4,128)(2,1)}, u32[]{:S(2)}) copy-start(bf16[2,4,576]{2,1,0:T(4,128)(2,1)} %new_ref.1) | copy-start | bytes 27652
  2.4 3.2 %copy-start.3 = (s32[2]{0:T(128)S(1)}, s32[2]{0:T(128)}, u32[]{:S(2)}) copy-start(s32[2]{0:T(128)} %lengths_ref.1) | copy-start | bytes 28
  2.4 3.2 %copy-start.4 = (s32[2]{0:T(128)S(1)}, s32[2]{0:T(128)}, u32[]{:S(2)}) copy-start(s32[2]{0:T(128)} %rows_ref.1) | copy-start | bytes 28
  5.6 1.3 %copy-start = (bf16[2,4,128,576]{3,2,1,0:T(8,128)(2,1)S(1)}, bf16[2,4,128,576]{3,2,1,0:T(8,128)(2,1)}, u32[]{:S(2)}) copy-start(bf16[2,4,128,576]{3,2,1,0:T(8,128)(2,1)} %copy.7.q_hbm) | copy-start | bytes 3538948
  6.9 1.2 %copy-start.1 = (bf16[8,512,128]{2,1,0:T(8,128)(2,1)S(1)}, bf16[8,512,128]{2,1,0:T(8,128)(2,1)}, u32[]{:S(2)}) copy-start(bf16[8,512,128]{2,1,0:T(8,128)(2,1)} %up_hbm.1) | copy-start | bytes 3145732

commit v2 on v1

--- a/solution.py
+++ b/solution.py
@@ -46,8 +46,8 @@
 ):
     rep = lax.axis_index("rep")
     me = lax.axis_index("tp")
-    slots, drafts, heads, _ = q_ref.shape
-    ctx = cache_ref.shape[1]
+    slots, drafts, _, heads = q_ref.shape
+    ctx = cache_ref.shape[2]
     lat, values = up_hbm.shape[1], up_hbm.shape[2]
     own_heads = up_hbm.shape[0]
     pairs = drafts // 2
@@ -82,12 +82,11 @@
     rows_out[...] = jnp.where((lane // (2 * own_heads)) % 2 == 0, rows_ref[0], rows_ref[1])
 
     def attend(b, pair):
-        q = q_ref[b, pl.ds(2 * pair, 2)].reshape(2 * heads, q_ref.shape[3])
+        q = jnp.concatenate([q_ref[b, 2 * pair], q_ref[b, 2 * pair + 1]], axis=1)
         keys = cache_ref[b]
         fresh = new_ref[b]
-        contract = (((1,), (1,)), ((), ()))
-        old = lax.dot_general(q, keys, contract, preferred_element_type=jnp.float32)
-        new = lax.dot_general(q, fresh, contract, preferred_element_type=jnp.float32)
+        old = lax.dot_general(q, keys, (((0,), (0,)), ((), ())), preferred_element_type=jnp.float32)
+        new = lax.dot_general(q, fresh, (((0,), (1,)), ((), ())), preferred_element_type=jnp.float32)
         position = lax.broadcasted_iota(jnp.int32, (1, ctx), 1)
         old = jnp.where(position < lengths_ref[b], old, -jnp.inf)
         step = 2 * pair + lax.broadcasted_iota(jnp.int32, new.shape, 0) // heads
@@ -96,7 +95,9 @@
         old = jnp.exp2((old - top) * scale)
         new = jnp.exp2((new - top) * scale)
         total = jnp.sum(old, axis=1, keepdims=True) + jnp.sum(new, axis=1, keepdims=True)
-        mixed = jnp.dot(old.astype(jnp.bfloat16), keys[:, :lat], preferred_element_type=jnp.float32)
+        mixed = lax.dot_general(
+            old.astype(jnp.bfloat16), keys[:lat], (((1,), (1,)), ((), ())), preferred_element_type=jnp.float32
+        )
         mixed = mixed + jnp.dot(new.astype(jnp.bfloat16), fresh[:, :lat], preferred_element_type=jnp.float32)
         latents = mixed * (1.0 / total)
         latents = latents.reshape(2, n, own_heads, lat)
@@ -243,8 +244,8 @@
         in_specs=[smem, smem, hbm, hbm, vmem, hbm],
         out_specs=vmem,
         scratch_shapes=[
-            pltpu.VMEM((slots, drafts, heads, embed), bf16),
-            pltpu.VMEM((slots, ctx, embed), bf16),
+            pltpu.VMEM((slots, drafts, embed, heads), bf16),
+            pltpu.VMEM((slots, embed, ctx), bf16),
             pltpu.VMEM((lat, own_heads * values), bf16),
             pltpu.VMEM((pairs, n, per_block, lat), bf16),
             pltpu.VMEM((pairs, n, per_block, lat), bf16),
@@ -262,8 +263,8 @@
             dma((pairs,)),
             dma((pairs,)),
         ],
-        compiler_params=pltpu.CompilerParams(collective_id=0, has_side_effects=True, vmem_limit_bytes=48 << 20),
-    )(cached_lengths, slot_rows, queries, latent_cache, new_latent, up_weight)
+        compiler_params=pltpu.CompilerParams(collective_id=0, has_side_effects=True, vmem_limit_bytes=60 << 20),
+    )(cached_lengths, slot_rows, queries.swapaxes(2, 3), latent_cache.swapaxes(1, 2), new_latent, up_weight)
     return out.reshape(slots, drafts, heads * values)
 
 

time: 52.5 us -> 46.1 us (0.88)
  local copies, waits for them, and re-layouts: 8.87 us -> 1.75 us
  Pallas kernels: 43.3 us -> 44.2 us
    unnamed x12 -> x0, local copies, waits for them, and re-layouts: 8.07 us -> none
    reshape x1, local copies, waits for them, and re-layouts: 0.8 us -> 1.75 us  [per_device(): return out.reshape(slots, drafts, heads * values)]
    pallas_call x1, Pallas kernels: 43.3 us -> 44.2 us  [per_device(): pl.pallas_call(functools.partial(kernel, n), out_shape=jax.ShapeDtypeStru...]
where the time goes in v2:
time: 46.1 us; the launch traced here: 45.9 us
  Pallas kernels  44.2 us (96%)
  local copies, waits for them, and re-layouts  1.75 us (4%)
    pallas_call x1, Pallas kernels, per_device(): pl.pallas_call(functools.partial(kernel, n), out_shape=jax.ShapeDtypeStru...  44.2 us
    reshape x1, local copies, waits for them, and re-layouts, per_device(): return out.reshape(slots, drafts, heads * values)  1.75 us

profile of v2, /device:TPU:1, one launch (start us, length us, event | category | flops | bytes accessed | tf_op | source)
XLA Modules:
  0.0 45.9 jit_solution(12762546724628472508)
XLA Ops:
  0.0 44.2 %shard_map.64 = bf16[8,16384]{1,0:T(8,128)(2,1)} custom-call(s32[2]{0:T(128)} %lengths_ref.1, s32[2]{0:T(128)} %rows_ref.1, bf16[2,4,576,128]{3,2,1,0:T(8,128)(2,1)} %bitcast.3, bf16[2,576,1024]{2,1,0:T(8,128)(2,1)} %bitcast.2, bf16[2,4,576]{2,1,0:T(4,128)(2,1)} %new_ref.1, bf16[8,512,128]{2,1,0:T(8,128)(2,1)} %up_hbm.1), custom_call_target="tpu_custom_call" | custom-call | tf_op jit(solution)/shard_map/pallas_call | solution.py:241
  44.2 1.8 %reshape.3 = bf16[2,4,16384]{2,1,0:T(4,128)(2,1)} reshape(bf16[8,16384]{1,0:T(8,128)(2,1)} %shard_map.64) | data formatting | bytes 524288 | tf_op jit(solution)/shard_map/reshape | solution.py:268

commit v3 on v2

--- a/solution.py
+++ b/solution.py
@@ -43,6 +43,7 @@
     send2_sem,
     recv2_sem,
     own2_sem,
+    ready_sem,
 ):
     rep = lax.axis_index("rep")
     me = lax.axis_index("tp")
@@ -56,9 +57,18 @@
     group_rows = PER_GROUP * per_block
     scale = (NOPE + ROPE) ** -0.5 * math.log2(math.e)
 
+    core = me % 2
     barrier = pltpu.get_barrier_semaphore()
-    for k in range(1, n):
-        pl.semaphore_signal(barrier, inc=1, device_id=(rep, (me + k) % n), device_id_type=MESH)
+
+    def announce(semaphore, offsets):
+        for k in offsets:
+            pl.semaphore_signal(semaphore, inc=1, device_id=(rep, (me + k) % n), device_id_type=MESH)
+
+    announce(barrier, range(2, n, 2))
+
+    @pl.when(core == 1)
+    def _():
+        announce(barrier, range(1, n, 2))
 
     loads = []
     for b in range(slots):
@@ -78,8 +88,11 @@
         copy.start()
         up_loads.append(copy)
 
-    lane = lax.broadcasted_iota(jnp.int32, (8, 128), 1)
-    rows_out[...] = jnp.where((lane // (2 * own_heads)) % 2 == 0, rows_ref[0], rows_ref[1])
+    chunks = lat // 128
+    lines_slot = 2 * own_heads
+    per_slot = lines_slot * chunks
+    lane = lax.broadcasted_iota(jnp.int32, (1, 128), 1)
+    rows_out[...] = jnp.where((lane // lines_slot) % 2 == 0, rows_ref[0], rows_ref[1])
 
     def attend(b, pair):
         q = jnp.concatenate([q_ref[b, 2 * pair], q_ref[b, 2 * pair + 1]], axis=1)
@@ -102,21 +115,38 @@
         latents = mixed * (1.0 / total)
         latents = latents.reshape(2, n, own_heads, lat)
         for d in range(n):
-            block = jnp.concatenate([latents[0, d], latents[1, d]], axis=0)
-            send1[pair, d, pl.ds(b * 2 * own_heads, 2 * own_heads), :] = block.astype(jnp.bfloat16)
-
-    def send_first(pair):
+            block = jnp.concatenate([latents[0, d], latents[1, d]], axis=0).astype(jnp.bfloat16)
+            for c in range(chunks):
+                send1[pair, d, pl.ds(b * per_slot + c * lines_slot, lines_slot), :] = block[:, c * 128 : (c + 1) * 128]
+
+    def send_first(pair, odd, first, last):
+        part = pl.ds(first, last - first)
         for p, k in enumerate(ORDER):
             to = (me + k) % n
+            if k % 2 != odd:
+                continue
             if k == 0:
-                pltpu.make_async_copy(send1.at[pair, me], recv1.at[pair, p], own1_sem.at[pair]).start()
-            else:
+                if last == slots * per_slot:
+                    pltpu.make_async_copy(send1.at[pair, me], recv1.at[pair, p], own1_sem.at[pair]).start()
+                continue
+            pltpu.make_async_remote_copy(
+                src_ref=send1.at[pair, to, part],
+                dst_ref=recv1.at[pair, p, part],
+                send_sem=send1_sem.at[pair],
+                recv_sem=recv1_sem.at[pair, p // PER_GROUP],
+                device_id=(rep, to),
+                device_id_type=MESH,
+            ).start()
+
+    def send_rows(odd):
+        for p, k in enumerate(ORDER):
+            if k and k % 2 == odd:
                 pltpu.make_async_remote_copy(
-                    src_ref=send1.at[pair, to],
-                    dst_ref=recv1.at[pair, p],
-                    send_sem=send1_sem.at[pair],
-                    recv_sem=recv1_sem.at[pair, p // PER_GROUP],
-                    device_id=(rep, to),
+                    src_ref=rows_out,
+                    dst_ref=rows_in.at[p],
+                    send_sem=rows_send_sem,
+                    recv_sem=rows_recv_sem,
+                    device_id=(rep, (me + k) % n),
                     device_id_type=MESH,
                 ).start()
 
@@ -126,24 +156,42 @@
                 for copy in loads[b]:
                     copy.wait()
             attend(b, pair)
-        if pair == 0:
-            pl.semaphore_wait(barrier, n - 1)
-            for p, k in enumerate(ORDER):
-                if k:
-                    pltpu.make_async_remote_copy(
-                        src_ref=rows_out,
-                        dst_ref=rows_in.at[p],
-                        send_sem=rows_send_sem,
-                        recv_sem=rows_recv_sem,
-                        device_id=(rep, (me + k) % n),
-                        device_id_type=MESH,
-                    ).start()
-        send_first(pair)
+            if pair == 0 and b == 0:
+                pl.semaphore_wait(barrier, n // 2 - 1 + (n // 2) * (1 - core))
+
+                @pl.when(core == 0)
+                def _():
+                    announce(ready_sem, range(1, n, 2))
+
+            if pair == 0:
+                first, last = b * per_slot, (b + 1) * per_slot
+            elif b == slots - 1:
+                first, last = 0, slots * per_slot
+            else:
+                continue
+            send_first(pair, 0, first, last)
+
+            @pl.when(core == 0)
+            def _():
+                send_first(pair, 1, first, last)
+
+            if pair == 0 and b == 0:
+                send_rows(0)
+
+                @pl.when(core == 0)
+                def _():
+                    send_rows(1)
+
+    @pl.when(core == 1)
+    def _():
+        pl.semaphore_wait(ready_sem, n // 2)
+        for pair in range(pairs):
+            send_first(pair, 1, 0, slots * per_slot)
+            if pair == 0:
+                send_rows(1)
 
     for copy in up_loads:
         copy.wait()
-    pltpu.make_async_copy(rows_in.at[pl.ds(0, n - 1)], rows_in.at[pl.ds(0, n - 1)], rows_recv_sem).wait()
-    rows_in[n - 1] = rows_out[...]
 
     out_lines = n * 16
     o = lax.broadcasted_iota(jnp.int32, (out_lines, group_rows), 0)
@@ -152,11 +200,14 @@
     same_draft = (o % 2) == (i // own_heads) % 2
     source = lax.broadcasted_iota(jnp.int32, (1, group_rows), 1) // per_block
     picks = []
-    for g in range(groups):
-        held = rows_in[g * PER_GROUP][0:1]
+    pltpu.make_async_copy(rows_in.at[pl.ds(0, n - 1)], rows_in.at[pl.ds(0, n - 1)], rows_recv_sem).wait()
+    rows_in[n - 1] = rows_out[...]
+
+    def pick(g):
+        held = rows_in[g * PER_GROUP]
         for s in range(1, PER_GROUP):
-            held = jnp.where(source == s, rows_in[g * PER_GROUP + s][0:1], held)
-        picks.append(jnp.where((want == held) & same_draft, 1.0, 0.0).astype(jnp.bfloat16))
+            held = jnp.where(source == s, rows_in[g * PER_GROUP + s], held)
+        return jnp.where((want == held) & same_draft, 1.0, 0.0).astype(jnp.bfloat16)
 
     line_head = lax.broadcasted_iota(jnp.int32, (group_rows, values), 0) % own_heads
     quarter = (lax.broadcasted_iota(jnp.int32, (out_lines, 256), 0) // 4) % 4
@@ -170,7 +221,11 @@
             pltpu.make_async_copy(arrived, arrived, recv1_sem.at[pair, g]).wait()
             if count < PER_GROUP:
                 pltpu.make_async_copy(send1.at[pair, me], recv1.at[pair, n - 1], own1_sem.at[pair]).wait()
-            block = recv1[pair, pl.ds(first, PER_GROUP)].reshape(group_rows, lat)
+            if pair == 0:
+                picks.append(pick(g))
+            block = recv1[pair, pl.ds(first, PER_GROUP)]
+            block = block.reshape(PER_GROUP * slots, chunks, lines_slot, 128)
+            block = jnp.concatenate([block[:, c] for c in range(chunks)], axis=2).reshape(group_rows, lat)
             full = jnp.dot(block, up_ref[...], preferred_element_type=jnp.float32)
             kept = jnp.concatenate(
                 [
@@ -215,9 +270,8 @@
     final = jnp.dot(place, recv2[...], preferred_element_type=jnp.float32)
     for s in range(n):
         for t in range(4):
-            out_ref[:, pl.ds(s * 1024 + t * 256, 256)] = final[t * 8 : (t + 1) * 8, s * 256 : (s + 1) * 256].astype(
-                jnp.bfloat16
-            )
+            lines = final[t * 8 : (t + 1) * 8, s * 256 : (s + 1) * 256].astype(jnp.bfloat16)
+            out_ref[:, :, pl.ds(s * 1024 + t * 256, 256)] = lines.reshape(slots, drafts, 256)
 
     pltpu.make_async_copy(rows_in.at[pl.ds(0, n - 1)], rows_in.at[pl.ds(0, n - 1)], rows_send_sem).wait()
     for pair in range(pairs):
@@ -238,21 +292,21 @@
     hbm = pl.BlockSpec(memory_space=pl.ANY)
     dma = pltpu.SemaphoreType.DMA
     bf16 = jnp.bfloat16
-    out = pl.pallas_call(
+    return pl.pallas_call(
         functools.partial(kernel, n),
-        out_shape=jax.ShapeDtypeStruct((slots * drafts, heads * values), bf16),
+        out_shape=jax.ShapeDtypeStruct((slots, drafts, heads * values), bf16),
         in_specs=[smem, smem, hbm, hbm, vmem, hbm],
         out_specs=vmem,
         scratch_shapes=[
             pltpu.VMEM((slots, drafts, embed, heads), bf16),
             pltpu.VMEM((slots, embed, ctx), bf16),
             pltpu.VMEM((lat, own_heads * values), bf16),
-            pltpu.VMEM((pairs, n, per_block, lat), bf16),
-            pltpu.VMEM((pairs, n, per_block, lat), bf16),
+            pltpu.VMEM((pairs, n, per_block * lat // 128, 128), bf16),
+            pltpu.VMEM((pairs, n, per_block * lat // 128, 128), bf16),
             pltpu.VMEM((pairs, n, 16, 256), bf16),
             pltpu.VMEM((pairs * 16, n * 256), bf16),
-            pltpu.VMEM((8, 128), jnp.int32),
-            pltpu.VMEM((n, 8, 128), jnp.int32),
+            pltpu.VMEM((1, 128), jnp.int32),
+            pltpu.VMEM((n, 1, 128), jnp.int32),
             dma((2 * slots + own_heads,)),
             dma,
             dma,
@@ -262,10 +316,10 @@
             dma((pairs,)),
             dma((pairs,)),
             dma((pairs,)),
+            pltpu.SemaphoreType.REGULAR,
         ],
         compiler_params=pltpu.CompilerParams(collective_id=0, has_side_effects=True, vmem_limit_bytes=60 << 20),
     )(cached_lengths, slot_rows, queries.swapaxes(2, 3), latent_cache.swapaxes(1, 2), new_latent, up_weight)
-    return out.reshape(slots, drafts, heads * values)
 
 
 def solution(mesh):

time: 46.1 us -> 43.2 us (0.937)
  Pallas kernels: 44.2 us -> 41.3 us
    pallas_call x1, Pallas kernels: 44.2 us -> 41.3 us  [per_device(): pl.pallas_call(functools.partial(kernel, n), out_shape=jax.ShapeDtypeStru...]
    reshape x1 -> x0, local copies, waits for them, and re-layouts: 1.75 us -> none  [per_device(): return out.reshape(slots, drafts, heads * values)]
    unnamed x0 -> x1, local copies, waits for them, and re-layouts: none -> 1.74 us
where the time goes in v3:
time: 43.2 us; the launch traced here: 43 us
  Pallas kernels  41.3 us (96%)
  local copies, waits for them, and re-layouts  1.74 us (4%)
    pallas_call x1, Pallas kernels, per_device(): pl.pallas_call(functools.partial(kernel, n), out_shape=jax.ShapeDtypeStru...  41.3 us
    unnamed x1, local copies, waits for them, and re-layouts  1.74 us

profile of v3, /device:TPU:1, one launch (start us, length us, event | category | flops | bytes accessed | tf_op | source)
XLA Modules:
  0.0 43.0 jit_solution(11055142965402748464)
XLA Ops:
  0.0 41.3 %shard_map.64 = bf16[2,4,16384]{2,1,0:T(4,128)(2,1)} custom-call(s32[2]{0:T(128)} %lengths_ref.1, s32[2]{0:T(128)} %rows_ref.1, bf16[2,4,576,128]{3,2,1,0:T(8,128)(2,1)} %bitcast.3, bf16[2,576,1024]{2,1,0:T(8,128)(2,1)} %bitcast.2, bf16[2,4,576]{2,1,0:T(4,128)(2,1)} %new_ref.1, bf16[8,512,128]{2,1,0:T(8,128)(2,1)} %up_hbm.1), custom_call_target="tpu_custom_call" | custom-call | tf_op jit(solution)/shard_map/pallas_call | solution.py:295
  41.3 1.7 %copy.8 = bf16[2,4,16384]{2,1,0:T(4,128)(2,1)} copy(bf16[2,4,16384]{2,1,0:T(4,128)(2,1)} %shard_map.64) | data formatting | bytes 524288

commit v4 on v3

--- a/solution.py
+++ b/solution.py
@@ -14,17 +14,22 @@
 
 ORDER = (8, 9, 7, 10, 6, 11, 5, 12, 4, 13, 3, 14, 2, 15, 1, 0)
 PER_GROUP = 4
+EARLY = (1, 0, 2, 3)
+EARLY_PAIRS = (1,)
 
 
 def kernel(
     n,
+    lengths_hbm,
+    rows_hbm,
+    q_hbm,
+    cache_hbm,
+    new_hbm,
+    up_hbm,
+    out_ref,
     lengths_ref,
     rows_ref,
-    q_hbm,
-    cache_hbm,
     new_ref,
-    up_hbm,
-    out_ref,
     q_ref,
     cache_ref,
     up_ref,
@@ -34,6 +39,7 @@
     recv2,
     rows_out,
     rows_in,
+    small_sem,
     load_sem,
     rows_send_sem,
     rows_recv_sem,
@@ -70,6 +76,10 @@
     def _():
         announce(barrier, range(1, n, 2))
 
+    small = []
+    for i, (src, dst) in enumerate(((lengths_hbm, lengths_ref), (new_hbm, new_ref), (rows_hbm, rows_ref))):
+        small.append(pltpu.make_async_copy(src, dst, small_sem.at[i]))
+        small[-1].start()
     loads = []
     for b in range(slots):
         loads.append(
@@ -78,20 +88,22 @@
                 pltpu.make_async_copy(q_hbm.at[b], q_ref.at[b], load_sem.at[2 * b + 1]),
             )
         )
-        for copy in loads[-1]:
-            copy.start()
+        if b == 0:
+            for copy in loads[-1]:
+                copy.start()
     up_loads = []
     for h in range(own_heads):
         copy = pltpu.make_async_copy(
             up_hbm.at[h], up_ref.at[:, pl.ds(h * values, values)], load_sem.at[2 * slots + h]
         )
-        copy.start()
         up_loads.append(copy)
 
     chunks = lat // 128
     lines_slot = 2 * own_heads
     per_slot = lines_slot * chunks
     lane = lax.broadcasted_iota(jnp.int32, (1, 128), 1)
+    for copy in small:
+        copy.wait()
     rows_out[...] = jnp.where((lane // lines_slot) % 2 == 0, rows_ref[0], rows_ref[1])
 
     def attend(b, pair):
@@ -155,6 +167,9 @@
             if pair == 0:
                 for copy in loads[b]:
                     copy.wait()
+                if b == 0:
+                    for copy in [*loads[1], *up_loads]:
+                        copy.start()
             attend(b, pair)
             if pair == 0 and b == 0:
                 pl.semaphore_wait(barrier, n // 2 - 1 + (n // 2) * (1 - core))
@@ -242,19 +257,27 @@
         send2[pair] = block.astype(jnp.bfloat16).reshape(n, 16, 256)
         columns = pl.ds(pl.multiple_of(me * 256, 256), 256)
         landing = recv2.at[pl.ds(pair * 16, 16), columns]
-        for k in ORDER:
+        pltpu.make_async_copy(send2.at[pair, me], landing, own2_sem.at[pair]).start()
+
+        def send_second(to):
+            pltpu.make_async_remote_copy(
+                src_ref=send2.at[pair, to],
+                dst_ref=landing,
+                send_sem=send2_sem.at[pair],
+                recv_sem=recv2_sem.at[pair],
+                device_id=(rep, to),
+                device_id_type=MESH,
+            ).start()
+
+        ahead = EARLY if pair in EARLY_PAIRS else ()
+        for to in ahead:
+            pl.when(me != to)(functools.partial(send_second, to))
+        for k in ORDER[:-1]:
             to = (me + k) % n
-            if k == 0:
-                pltpu.make_async_copy(send2.at[pair, me], landing, own2_sem.at[pair]).start()
+            if ahead:
+                pl.when(to >= len(ahead))(functools.partial(send_second, to))
             else:
-                pltpu.make_async_remote_copy(
-                    src_ref=send2.at[pair, to],
-                    dst_ref=landing,
-                    send_sem=send2_sem.at[pair],
-                    recv_sem=recv2_sem.at[pair],
-                    device_id=(rep, to),
-                    device_id_type=MESH,
-                ).start()
+                send_second(to)
 
     for pair in range(pairs):
         arrived = recv2.at[pl.ds(pair * 16, 16), pl.ds(0, (n - 1) * 256)]
@@ -287,17 +310,19 @@
     ctx = latent_cache.shape[1]
     pairs = drafts // 2
     per_block = slots * 2 * own_heads
-    smem = pl.BlockSpec(memory_space=pltpu.SMEM)
     vmem = pl.BlockSpec(memory_space=pltpu.VMEM)
     hbm = pl.BlockSpec(memory_space=pl.ANY)
     dma = pltpu.SemaphoreType.DMA
     bf16 = jnp.bfloat16
     return pl.pallas_call(
         functools.partial(kernel, n),
-        out_shape=jax.ShapeDtypeStruct((slots, drafts, heads * values), bf16),
-        in_specs=[smem, smem, hbm, hbm, vmem, hbm],
+        out_shape=pltpu.VMEM((slots, drafts, heads * values), bf16),
+        in_specs=[hbm] * 6,
         out_specs=vmem,
         scratch_shapes=[
+            pltpu.SMEM((slots,), jnp.int32),
+            pltpu.SMEM((slots,), jnp.int32),
+            pltpu.VMEM((slots, drafts, embed), bf16),
             pltpu.VMEM((slots, drafts, embed, heads), bf16),
             pltpu.VMEM((slots, embed, ctx), bf16),
             pltpu.VMEM((lat, own_heads * values), bf16),
@@ -307,6 +332,7 @@
             pltpu.VMEM((pairs * 16, n * 256), bf16),
             pltpu.VMEM((1, 128), jnp.int32),
             pltpu.VMEM((n, 1, 128), jnp.int32),
+            dma((3,)),
             dma((2 * slots + own_heads,)),
             dma,
             dma,

time: 43.2 us -> 40.3 us (0.933)
  Pallas kernels: 41.3 us -> 39.4 us
  local copies, waits for them, and re-layouts: 1.74 us -> 0.71 us
    pallas_call x1, Pallas kernels: 41.3 us -> 39.4 us  [per_device(): pl.pallas_call(functools.partial(kernel, n), out_shape=pltpu.VMEM((slots,...]
    unnamed x1, local copies, waits for them, and re-layouts: 1.74 us -> 0.71 us
where the time goes in v4:
time: 40.3 us; the launch traced here: 40.2 us
  Pallas kernels  39.4 us (98%)
  local copies, waits for them, and re-layouts  0.71 us (2%)
    pallas_call x1, Pallas kernels, per_device(): pl.pallas_call(functools.partial(kernel, n), out_shape=pltpu.VMEM((slots,...  39.4 us

profile of v4, /device:TPU:1, one launch (start us, length us, event | category | flops | bytes accessed | tf_op | source)
XLA Modules:
  0.0 40.2 jit_solution(14887866003276946210)
XLA Ops:
  0.0 39.4 %shard_map.64 = bf16[2,4,16384]{2,1,0:T(4,128)(2,1)S(1)} custom-call(s32[2]{0:T(128)} %lengths_hbm.1, s32[2]{0:T(128)} %rows_hbm.1, bf16[2,4,576,128]{3,2,1,0:T(8,128)(2,1)} %bitcast.3, bf16[2,576,1024]{2,1,0:T(8,128)(2,1)} %bitcast.2, bf16[2,4,576]{2,1,0:T(4,128)(2,1)} %new_hbm.1, bf16[8,512,128]{2,1,0:T(8,128)(2,1)} %up_hbm.1), custom_call_target="tpu_custom_call" | custom-call | tf_op jit(solution)/shard_map/pallas_call | solution.py:317
  39.5 0.7 %copy.8 = bf16[2,4,16384]{2,1,0:T(4,128)(2,1)} copy(bf16[2,4,16384]{2,1,0:T(4,128)(2,1)S(1)} %shard_map.64) | data formatting | bytes 524288

commit v5 on v4

--- a/solution.py
+++ b/solution.py
@@ -63,23 +63,6 @@
     group_rows = PER_GROUP * per_block
     scale = (NOPE + ROPE) ** -0.5 * math.log2(math.e)
 
-    core = me % 2
-    barrier = pltpu.get_barrier_semaphore()
-
-    def announce(semaphore, offsets):
-        for k in offsets:
-            pl.semaphore_signal(semaphore, inc=1, device_id=(rep, (me + k) % n), device_id_type=MESH)
-
-    announce(barrier, range(2, n, 2))
-
-    @pl.when(core == 1)
-    def _():
-        announce(barrier, range(1, n, 2))
-
-    small = []
-    for i, (src, dst) in enumerate(((lengths_hbm, lengths_ref), (new_hbm, new_ref), (rows_hbm, rows_ref))):
-        small.append(pltpu.make_async_copy(src, dst, small_sem.at[i]))
-        small[-1].start()
     loads = []
     for b in range(slots):
         loads.append(
@@ -88,9 +71,26 @@
                 pltpu.make_async_copy(q_hbm.at[b], q_ref.at[b], load_sem.at[2 * b + 1]),
             )
         )
-        if b == 0:
-            for copy in loads[-1]:
-                copy.start()
+    for copy in loads[0]:
+        copy.start()
+
+    core = me % 2
+    barrier = pltpu.get_barrier_semaphore()
+
+    def announce(semaphore, offsets):
+        for k in offsets:
+            pl.semaphore_signal(semaphore, inc=1, device_id=(rep, (me + k) % n), device_id_type=MESH)
+
+    announce(barrier, [k for k in ORDER[:-1] if k % 2 == 0])
+
+    @pl.when(core == 1)
+    def _():
+        announce(barrier, [k for k in ORDER if k % 2])
+
+    small = []
+    for i, (src, dst) in enumerate(((lengths_hbm, lengths_ref), (new_hbm, new_ref), (rows_hbm, rows_ref))):
+        small.append(pltpu.make_async_copy(src, dst, small_sem.at[i]))
+        small[-1].start()
     up_loads = []
     for h in range(own_heads):
         copy = pltpu.make_async_copy(
@@ -162,6 +162,14 @@
                     device_id_type=MESH,
                 ).start()
 
+    def meet():
+        pl.semaphore_wait(barrier, n // 2 - 1 + (n // 2) * (1 - core))
+
+        @pl.when(core == 0)
+        def _():
+            announce(ready_sem, [k for k in ORDER if k % 2])
+
+    pl.when(me == 0)(meet)
     for pair in range(pairs):
         for b in range(slots):
             if pair == 0:
@@ -172,11 +180,7 @@
                         copy.start()
             attend(b, pair)
             if pair == 0 and b == 0:
-                pl.semaphore_wait(barrier, n // 2 - 1 + (n // 2) * (1 - core))
-
-                @pl.when(core == 0)
-                def _():
-                    announce(ready_sem, range(1, n, 2))
+                pl.when(me != 0)(meet)
 
             if pair == 0:
                 first, last = b * per_slot, (b + 1) * per_slot

time: 40.3 us -> 40 us (level)
  no operation moved by 1% of the time
where the time goes in v5:
time: 40 us; the launch traced here: 39.9 us
  Pallas kernels  39.2 us (98%)
  local copies, waits for them, and re-layouts  0.71 us (2%)
    pallas_call x1, Pallas kernels, per_device(): pl.pallas_call(functools.partial(kernel, n), out_shape=pltpu.VMEM((slots,...  39.2 us

profile of v5, /device:TPU:1, one launch (start us, length us, event | category | flops | bytes accessed | tf_op | source)
XLA Modules:
  0.0 39.9 jit_solution(2890072548780329036)
XLA Ops:
  0.0 39.2 %shard_map.64 = bf16[2,4,16384]{2,1,0:T(4,128)(2,1)S(1)} custom-call(s32[2]{0:T(128)} %lengths_hbm.1, s32[2]{0:T(128)} %rows_hbm.1, bf16[2,4,576,128]{3,2,1,0:T(8,128)(2,1)} %bitcast.3, bf16[2,576,1024]{2,1,0:T(8,128)(2,1)} %bitcast.2, bf16[2,4,576]{2,1,0:T(4,128)(2,1)} %new_hbm.1, bf16[8,512,128]{2,1,0:T(8,128)(2,1)} %up_hbm.1), custom_call_target="tpu_custom_call" | custom-call | tf_op jit(solution)/shard_map/pallas_call | solution.py:321
  39.2 0.7 %copy.8 = bf16[2,4,16384]{2,1,0:T(4,128)(2,1)} copy(bf16[2,4,16384]{2,1,0:T(4,128)(2,1)S(1)} %shard_map.64) | data formatting | bytes 524288

commit v6 on v5

--- a/solution.py
+++ b/solution.py
@@ -194,7 +194,7 @@
             def _():
                 send_first(pair, 1, first, last)
 
-            if pair == 0 and b == 0:
+            if pair == 0 and b == slots - 1:
                 send_rows(0)
 
                 @pl.when(core == 0)

time: 40 us -> 40 us (level)
  no operation moved by 1% of the time
where the time goes in v6:
time: 40 us; the launch traced here: 39.9 us
  Pallas kernels  39.2 us (98%)
  local copies, waits for them, and re-layouts  0.71 us (2%)
    pallas_call x1, Pallas kernels, per_device(): pl.pallas_call(functools.partial(kernel, n), out_shape=pltpu.VMEM((slots,...  39.2 us

profile of v6, /device:TPU:1, one launch (start us, length us, event | category | flops | bytes accessed | tf_op | source)
XLA Modules:
  0.0 39.9 jit_solution(10218027655925210063)
XLA Ops:
  0.0 39.2 %shard_map.64 = bf16[2,4,16384]{2,1,0:T(4,128)(2,1)S(1)} custom-call(s32[2]{0:T(128)} %lengths_hbm.1, s32[2]{0:T(128)} %rows_hbm.1, bf16[2,4,576,128]{3,2,1,0:T(8,128)(2,1)} %bitcast.3, bf16[2,576,1024]{2,1,0:T(8,128)(2,1)} %bitcast.2, bf16[2,4,576]{2,1,0:T(4,128)(2,1)} %new_hbm.1, bf16[8,512,128]{2,1,0:T(8,128)(2,1)} %up_hbm.1), custom_call_target="tpu_custom_call" | custom-call | tf_op jit(solution)/shard_map/pallas_call | solution.py:321
  39.2 0.7 %copy.8 = bf16[2,4,16384]{2,1,0:T(4,128)(2,1)} copy(bf16[2,4,16384]{2,1,0:T(4,128)(2,1)S(1)} %shard_map.64) | data formatting | bytes 524288
